TPU v7x, 32 devices: a whole 2x2x4 slice. The times are simulated.
32 devices in a mesh: group: 2 (over y), tm: 4 (over z), mode: 2 (over x), col: 2 (over core).
Axes of the slice: x: 2, y: 2, z: 4, core: 2. Of those that a mesh axis runs over, the one named last changes fastest.
Arguments:
- flags: int32 [32], P(('group', 'tm')), parts along dimension 0, may hold values 0 or 1
- base_load: bfloat16 [32, 32, 1024], P(('group', 'tm'), 'col', 'mode'), parts along dimension 0, may hold values from -0.29882812 to 0.29882812
- solar_load: bfloat16 [64, 1024], P(('group', 'col'), 'mode'), parts along dimension 0, may hold values from -0.29882812 to 0.29882812
- target: bfloat16 [32, 32, 1024], P(('group', 'tm'), 'col', 'mode'), parts along dimension 0, may hold values from -6 to 6
- coarse_state: float32 [8, 32, 1024], P(('group', 'tm'), 'col', 'mode'), parts along dimension 0, may hold values from -6 to 6
- adjoint_state: float32 [8, 32, 1024], P(('group', 'tm'), 'col', 'mode'), parts along dimension 0, may hold values from -6 to 6
- step_sun: bfloat16 [1024, 1024], P('mode'), may hold values from -1 to 1
- step_eclipse: bfloat16 [1024, 1024], P('mode'), may hold values from -1 to 1
- coarse_step: bfloat16 [1024, 1024], P('mode'), may hold values from -1 to 1
Outputs:
- trajectory: float32 [32, 32, 1024], P(('group', 'tm'), 'col', 'mode'), parts along dimension 0
- adjoint_path: float32 [32, 32, 1024], P(('group', 'tm'), 'col', 'mode'), parts along dimension 0
There are 2 independent parts, one for each index of `group`. A program takes and returns all parts, laid end to end along the dimension named above; an argument that names none is the same for every part. Nothing has to cross between parts.
All inputs are finite; a program needn't handle non-finite values. No bound on the sum of `flags` on one device may be relied on, other than what follows from the above.
Results may differ from a plain program's by a relative error of at most 0.0026.
Values may be sent and summed in bfloat16 or wider, within the bound.
A program may use at most 64 MiB of HBM per device.

v0:
```python
import jax
import jax.numpy as jnp
from jax import lax
from jax.sharding import PartitionSpec as P

OBJ_WEIGHT = 0.0625
EXACT = lax.Precision.HIGHEST


def from_behind(block, axis, distance):
    devices = range(lax.axis_size(axis))
    route = [(i - distance, i) for i in devices if i - distance in devices]
    return lax.ppermute(block, axis, route)


def pick_mats(flag_column, sun_part, eclipse_part):
    return jnp.where(flag_column[:, None, None] == 1, eclipse_part[None], sun_part[None])


def coarse_forward(error_rows, matrix_rows):
    gathered = lax.all_gather(error_rows, "mode", axis=1, tiled=True)
    return jnp.einsum("cm,rm->cr", gathered, matrix_rows, precision=EXACT)


def coarse_backward(error_rows, matrix_columns):
    gathered = lax.all_gather(error_rows, "mode", axis=1, tiled=True)
    return jnp.dot(gathered, matrix_columns, precision=EXACT)


def forward_prefix(offsets, advance):

    def forward_relay_turn(step, incoming):
        outgoing = advance(incoming) + offsets
        return from_behind(outgoing, "tm", 1)

    return lax.fori_loop(0, lax.axis_size("tm") - 1, forward_relay_turn, jnp.zeros_like(offsets))


def backward_prefix(offsets, advance):

    def backward_relay_turn(step, incoming):
        outgoing = advance(incoming) + offsets
        return from_behind(outgoing, "tm", -1)

    return lax.fori_loop(0, lax.axis_size("tm") - 1, backward_relay_turn, jnp.zeros_like(offsets))


def local(
    flags,
    base_load,
    solar_load,
    target,
    coarse_state,
    adjoint_state,
    step_sun,
    step_eclipse,
    coarse_step,
):
    intervals = coarse_state.shape[0]
    fine_count = flags.shape[0] // intervals
    tm_index = lax.axis_index("tm")
    flag_grid = flags.reshape(intervals, fine_count)
    load_here, target_here, solar_here = (base_load, target, solar_load[None])
    state_here, adjoint_here = (coarse_state, adjoint_state)
    sun_cols, eclipse_cols = (
        lax.all_to_all(step_sun, "mode", split_axis=1, concat_axis=0, tiled=True),
        lax.all_to_all(step_eclipse, "mode", split_axis=1, concat_axis=0, tiled=True),
    )
    coarse_full = lax.all_gather(coarse_step, "mode", axis=0, tiled=True).astype(jnp.float32)
    coarse_rows = coarse_step.astype(jnp.float32)
    mode_start = lax.axis_index("mode") * coarse_rows.shape[0]
    coarse_cols = lax.dynamic_slice_in_dim(coarse_full, mode_start, coarse_rows.shape[0], 1)
    power_cols = lax.all_to_all(coarse_rows, "mode", split_axis=1, concat_axis=0, tiled=True)

    def forward_product(current, position):
        gathered = lax.all_gather(current.astype(jnp.bfloat16), "mode", axis=2, tiled=True)
        mats = pick_mats(flag_grid[:, position], step_sun, step_eclipse)
        return jnp.einsum("icm,irm->icr", gathered, mats, preferred_element_type=jnp.float32)

    def backward_product(current, position):
        gathered = lax.all_gather(current.astype(jnp.bfloat16), "mode", axis=2, tiled=True)
        mats = pick_mats(flag_grid[:, position], sun_cols, eclipse_cols)
        return jnp.einsum("icm,imr->icr", gathered, mats, preferred_element_type=jnp.float32)

    def advance_up(value):
        return coarse_forward(value, coarse_rows)

    def advance_down(value):
        return coarse_backward(value, power_cols)

    col_count = state_here.shape[1]
    row_count = state_here.shape[2]
    load_grid = load_here.reshape(intervals, fine_count, col_count, row_count)
    solar = solar_here[0].astype(jnp.float32)

    def forcing(position):
        sun_on = (1 - flag_grid[:, position]).astype(jnp.float32)
        return load_grid[:, position].astype(jnp.float32) + sun_on[:, None, None] * solar[None]

    current = state_here
    for position in range(fine_count):
        current = forward_product(current, position) + forcing(position)
    arrived = from_behind(current[intervals - 1], "tm", 1)
    previous = jnp.concatenate([arrived[None], current[:-1]], 0)
    is_first = jnp.logical_and(tm_index == 0, jnp.arange(intervals) == 0)
    residual = jnp.where(is_first[:, None, None], 0.0, previous - state_here)
    partial_sum = residual[0]
    incoming = forward_prefix(partial_sum, advance_up)
    running = incoming
    index = 0
    running = coarse_forward(running, coarse_rows) + residual[index]
    corrections = [running]
    corrected = state_here + jnp.stack(corrections)
    current = corrected
    points = [corrected]
    for position in range(fine_count - 1):
        current = forward_product(current, position) + forcing(position)
        points.append(current)
    trajectory = jnp.stack(points, 1).reshape(intervals * fine_count, col_count, row_count)
    source = OBJ_WEIGHT * (trajectory - target_here.astype(jnp.float32))
    source_grid = source.reshape(intervals, fine_count, col_count, row_count)
    next_first = from_behind(adjoint_here[0], "tm", -1)
    starts = jnp.concatenate([adjoint_here[1:], next_first[None]], 0)
    current = starts
    for position in range(fine_count - 1, -1, -1):
        current = backward_product(current, position) + source_grid[:, position]
    back_residual = current - adjoint_here
    partial_back = back_residual[intervals - 1]
    incoming_back = backward_prefix(partial_back, advance_down)
    running = incoming_back
    back_list = {}
    index = 0
    running = coarse_backward(running, coarse_cols) + back_residual[index]
    back_list[index] = running
    back_corrected = adjoint_here + jnp.stack([back_list[0]])
    next_fixed = from_behind(back_corrected[0], "tm", -1)
    current = jnp.concatenate([back_corrected[1:], next_fixed[None]], 0)
    values = {0: back_corrected}
    for position in range(fine_count - 1, 0, -1):
        current = backward_product(current, position) + source_grid[:, position]
        values[position] = current
    adjoint_path = jnp.stack([values[position] for position in range(fine_count)], 1).reshape(
        intervals * fine_count, col_count, row_count
    )
    return (trajectory, adjoint_path)


def solution(mesh):
    in_specs = (
        P(("group", "tm")),
        P(("group", "tm"), "col", "mode"),
        P(("group", "col"), "mode"),
        P(("group", "tm"), "col", "mode"),
        P(("group", "tm"), "col", "mode"),
        P(("group", "tm"), "col", "mode"),
        P("mode", None),
        P("mode", None),
        P("mode", None),
    )
    out_specs = (P(("group", "tm"), "col", "mode"), P(("group", "tm"), "col", "mode"))
    return jax.shard_map(local, mesh=mesh, in_specs=in_specs, out_specs=out_specs, check_vma=False)
```

profile of v0, /device:TPU:0, one launch (start us, length us, event | category | flops | bytes accessed | tf_op | source)
XLA Modules:
  0.0 235.5 jit_solution(13226086354550520769)
XLA Ops:
  14.4 5.3 %all_gather.57 = bf16[1,16,1024]{2,1,0:T(8,128)(2,1)S(1)} all-gather(bf16[1,16,512]{2,1,0:T(8,128)(2,1)S(1)} %convert_element_type.139), channel_id=1, replica_groups=mesh['group'=2,'tm'=4,'mode'=2,'col'=2] {'mode'}, dimensions={2}, use_global_device_ids=true | all-gather | bytes 49152 | tf_op jit(solution)/shard_map/all_gather | solution.py:76
  21.3 4.4 %all-gather = bf16[16,1024]{1,0:T(8,128)(2,1)S(1)} all-gather(bf16[16,512]{1,0:T(8,128)(2,1)S(1)} %fusion.11), channel_id=2, replica_groups=mesh['group'=2,'tm'=4,'mode'=2,'col'=2] {'mode'}, dimensions={1}, use_global_device_ids=true | all-gather | bytes 49152 | tf_op jit(solution)/shard_map/all_gather | solution.py:76
  26.1 4.4 %all-gather.1 = bf16[16,1024]{1,0:T(8,128)(2,1)S(1)} all-gather(bf16[16,512]{1,0:T(8,128)(2,1)S(1)} %fusion.12), channel_id=3, replica_groups=mesh['group'=2,'tm'=4,'mode'=2,'col'=2] {'mode'}, dimensions={1}, use_global_device_ids=true | all-gather | bytes 49152 | tf_op jit(solution)/shard_map/all_gather | solution.py:76
  30.9 4.4 %all-gather.2 = bf16[16,1024]{1,0:T(8,128)(2,1)S(1)} all-gather(bf16[16,512]{1,0:T(8,128)(2,1)S(1)} %fusion.13), channel_id=4, replica_groups=mesh['group'=2,'tm'=4,'mode'=2,'col'=2] {'mode'}, dimensions={1}, use_global_device_ids=true | all-gather | bytes 49152 | tf_op jit(solution)/shard_map/all_gather | solution.py:76
  42.4 4.4 %all-to-all-start.1 = ((bf16[512,2,512]{0,2,1:T(8,128)(2,1)}), bf16[512,2,512]{0,2,1:T(8,128)(2,1)}, u32[]{:S(2)}, u32[]{:S(2)}) async-start(bf16[512,2,512]{0,2,1:T(8,128)(2,1)} %bitcast.27), calls=%async_computation.1 | async-start | bytes 2097152 | tf_op jit(solution)/shard_map/all_to_all | solution.py:67
  52.9 4.4 %all-gather.5 = bf16[16,1024]{1,0:T(8,128)(2,1)S(1)} all-gather(bf16[16,512]{1,0:T(8,128)(2,1)S(1)} %collective-permute-done.3), channel_id=7, replica_groups=mesh['group'=2,'tm'=4,'mode'=2,'col'=2] {'mode'}, dimensions={1}, use_global_device_ids=true | all-gather | bytes 49152 | tf_op jit(solution)/shard_map/all_gather | solution.py:81
  57.3 38.2 %while.20 = (s32[]{:T(128)}, f32[16,512]{1,0:T(8,128)S(1)}, f32[512,1024]{1,0:T(8,128)S(1)}, f32[16,512]{1,0:T(8,128)S(1)}, s32[]{:T(128)}) while((s32[]{:T(128)}, f32[16,512]{1,0:T(8,128)S(1)}, f32[512,1024]{1,0:T(8,128)S(1)}, f32[16,512]{1,0:T(8,128)S(1)}, s32[]{:T(128)}) %tuple.47), condition=%wide.region_1.2_spmd, body=%wide.region_0.1_spmd.sunk | while | flops 100671488 | bytes 2457701 | solution.py:36
  57.3 4.6 %all_gather.76 = f32[16,1024]{1,0:T(8,128)S(1)} all-gather(f32[16,512]{1,0:T(8,128)S(1)} %get-tuple-element.140), channel_id=1, replica_groups=mesh['group'=2,'tm'=4,'mode'=2,'col'=2] {'mode'}, dimensions={1}, use_global_device_ids=true | all-gather | bytes 98304 | tf_op jit(solution)/shard_map/while/body/eval_jaxpr/all_gather | solution.py:21
  63.7 5.0 %collective-permute-start = (f32[16,512]{1,0:T(8,128)S(1)}, f32[16,512]{1,0:T(8,128)S(1)}, u32[]{:S(2)}, u32[]{:S(2)}) collective-permute-start(f32[16,512]{1,0:T(8,128)S(1)} %convolution_add_fusion.18), channel_id=1, source_target_pairs={{0,4},{4,8},{8,12},{1,5},{5,9},{9,13},{2,6},{6,10},{10,14},{3,7},{... | collective-permute-start | bytes 98312 | tf_op jit(solution)/shard_map/while/body/eval_jaxpr/ppermute | solution.py:13
  70.3 5.3 %all_gather.76 = f32[16,1024]{1,0:T(8,128)S(1)} all-gather(f32[16,512]{1,0:T(8,128)S(1)} %get-tuple-element.140), channel_id=1, replica_groups=mesh['group'=2,'tm'=4,'mode'=2,'col'=2] {'mode'}, dimensions={1}, use_global_device_ids=true | all-gather | bytes 98304 | tf_op jit(solution)/shard_map/while/body/eval_jaxpr/all_gather | solution.py:21
  77.5 4.2 %collective-permute-start = (f32[16,512]{1,0:T(8,128)S(1)}, f32[16,512]{1,0:T(8,128)S(1)}, u32[]{:S(2)}, u32[]{:S(2)}) collective-permute-start(f32[16,512]{1,0:T(8,128)S(1)} %convolution_add_fusion.18), channel_id=1, source_target_pairs={{0,4},{4,8},{8,12},{1,5},{5,9},{9,13},{2,6},{6,10},{10,14},{3,7},{... | collective-permute-start | bytes 98312 | tf_op jit(solution)/shard_map/while/body/eval_jaxpr/ppermute | solution.py:13
  83.3 4.6 %all_gather.76 = f32[16,1024]{1,0:T(8,128)S(1)} all-gather(f32[16,512]{1,0:T(8,128)S(1)} %get-tuple-element.140), channel_id=1, replica_groups=mesh['group'=2,'tm'=4,'mode'=2,'col'=2] {'mode'}, dimensions={1}, use_global_device_ids=true | all-gather | bytes 98304 | tf_op jit(solution)/shard_map/while/body/eval_jaxpr/all_gather | solution.py:21
  89.7 4.2 %collective-permute-start = (f32[16,512]{1,0:T(8,128)S(1)}, f32[16,512]{1,0:T(8,128)S(1)}, u32[]{:S(2)}, u32[]{:S(2)}) collective-permute-start(f32[16,512]{1,0:T(8,128)S(1)} %convolution_add_fusion.18), channel_id=1, source_target_pairs={{0,4},{4,8},{8,12},{1,5},{5,9},{9,13},{2,6},{6,10},{10,14},{3,7},{... | collective-permute-start | bytes 98312 | tf_op jit(solution)/shard_map/while/body/eval_jaxpr/ppermute | solution.py:13
  95.5 4.9 %all_gather.61 = f32[16,1024]{1,0:T(8,128)S(1)} all-gather(f32[16,512]{1,0:T(8,128)S(1)} %get-tuple-element.46), channel_id=1, replica_groups=mesh['group'=2,'tm'=4,'mode'=2,'col'=2] {'mode'}, dimensions={1}, use_global_device_ids=true | all-gather | bytes 98304 | tf_op jit(solution)/shard_map/all_gather | solution.py:21
  102.5 4.6 %all_gather.62 = bf16[1,16,1024]{2,1,0:T(8,128)(2,1)S(1)} all-gather(bf16[1,16,512]{2,1,0:T(8,128)(2,1)S(1)} %get-tuple-element.74), channel_id=1, replica_groups=mesh['group'=2,'tm'=4,'mode'=2,'col'=2] {'mode'}, dimensions={2}, use_global_device_ids=true | all-gather | bytes 49152 | tf_op jit(solution)/shard_map/all_gather | solution.py:76
  108.8 4.5 %all-gather.3 = bf16[16,1024]{1,0:T(8,128)(2,1)S(1)} all-gather(bf16[16,512]{1,0:T(8,128)(2,1)S(1)} %get-tuple-element.76), channel_id=5, replica_groups=mesh['group'=2,'tm'=4,'mode'=2,'col'=2] {'mode'}, dimensions={1}, use_global_device_ids=true | all-gather | bytes 49152 | tf_op jit(solution)/shard_map/all_gather | solution.py:76
  117.3 14.9 %all-gather.4 = bf16[16,1024]{1,0:T(8,128)(2,1)S(1)} all-gather(bf16[16,512]{1,0:T(8,128)(2,1)S(1)} %get-tuple-element.78), channel_id=6, replica_groups=mesh['group'=2,'tm'=4,'mode'=2,'col'=2] {'mode'}, dimensions={1}, use_global_device_ids=true | all-gather | bytes 49152 | tf_op jit(solution)/shard_map/all_gather | solution.py:76
  150.5 4.4 %all-gather.6 = bf16[16,1024]{1,0:T(8,128)(2,1)S(1)} all-gather(bf16[16,512]{1,0:T(8,128)(2,1)S(1)} %fusion.16), channel_id=8, replica_groups=mesh['group'=2,'tm'=4,'mode'=2,'col'=2] {'mode'}, dimensions={1}, use_global_device_ids=true | all-gather | bytes 49152 | tf_op jit(solution)/shard_map/all_gather | solution.py:81
  156.4 4.5 %all-gather.7 = bf16[16,1024]{1,0:T(8,128)(2,1)S(1)} all-gather(bf16[16,512]{1,0:T(8,128)(2,1)S(1)} %fusion.14), channel_id=9, replica_groups=mesh['group'=2,'tm'=4,'mode'=2,'col'=2] {'mode'}, dimensions={1}, use_global_device_ids=true | all-gather | bytes 49152 | tf_op jit(solution)/shard_map/all_gather | solution.py:81
  161.1 4.4 %all-gather.8 = bf16[16,1024]{1,0:T(8,128)(2,1)S(1)} all-gather(bf16[16,512]{1,0:T(8,128)(2,1)S(1)} %fusion.15), channel_id=10, replica_groups=mesh['group'=2,'tm'=4,'mode'=2,'col'=2] {'mode'}, dimensions={1}, use_global_device_ids=true | all-gather | bytes 49152 | tf_op jit(solution)/shard_map/all_gather | solution.py:81
  165.8 34.9 %while.21 = (s32[]{:T(128)}, f32[16,512]{1,0:T(8,128)S(1)}, f32[1024,512]{1,0:T(8,128)S(1)}, f32[16,512]{1,0:T(8,128)S(1)}, s32[]{:T(128)}) while((s32[]{:T(128)}, f32[16,512]{1,0:T(8,128)S(1)}, f32[1024,512]{1,0:T(8,128)S(1)}, f32[16,512]{1,0:T(8,128)S(1)}, s32[]{:T(128)}) %tuple.55), condition=%wide.region_3.4_spmd, body=%wide.region_2.3_spmd.sunk | while | flops 100671488 | bytes 2457701 | solution.py:45
  165.8 4.9 %all_gather.77 = f32[16,1024]{1,0:T(8,128)S(1)} all-gather(f32[16,512]{1,0:T(8,128)S(1)} %get-tuple-element.155), channel_id=1, replica_groups=mesh['group'=2,'tm'=4,'mode'=2,'col'=2] {'mode'}, dimensions={1}, use_global_device_ids=true | all-gather | bytes 98304 | tf_op jit(solution)/shard_map/while/body/eval_jaxpr/all_gather | solution.py:26
  173.1 4.6 %collective-permute-done.1 = f32[16,512]{1,0:T(8,128)S(1)} collective-permute-done((f32[16,512]{1,0:T(8,128)S(1)}, f32[16,512]{1,0:T(8,128)S(1)}, u32[]{:S(2)}, u32[]{:S(2)}) %collective-permute-start.1) | collective-permute-done | bytes 32800 | tf_op jit(solution)/shard_map/while/body/eval_jaxpr/ppermute | solution.py:13
  177.6 4.6 %all_gather.77 = f32[16,1024]{1,0:T(8,128)S(1)} all-gather(f32[16,512]{1,0:T(8,128)S(1)} %get-tuple-element.155), channel_id=1, replica_groups=mesh['group'=2,'tm'=4,'mode'=2,'col'=2] {'mode'}, dimensions={1}, use_global_device_ids=true | all-gather | bytes 98304 | tf_op jit(solution)/shard_map/while/body/eval_jaxpr/all_gather | solution.py:26
  184.6 4.5 %collective-permute-done.1 = f32[16,512]{1,0:T(8,128)S(1)} collective-permute-done((f32[16,512]{1,0:T(8,128)S(1)}, f32[16,512]{1,0:T(8,128)S(1)}, u32[]{:S(2)}, u32[]{:S(2)}) %collective-permute-start.1) | collective-permute-done | bytes 32800 | tf_op jit(solution)/shard_map/while/body/eval_jaxpr/ppermute | solution.py:13
  189.1 4.6 %all_gather.77 = f32[16,1024]{1,0:T(8,128)S(1)} all-gather(f32[16,512]{1,0:T(8,128)S(1)} %get-tuple-element.155), channel_id=1, replica_groups=mesh['group'=2,'tm'=4,'mode'=2,'col'=2] {'mode'}, dimensions={1}, use_global_device_ids=true | all-gather | bytes 98304 | tf_op jit(solution)/shard_map/while/body/eval_jaxpr/all_gather | solution.py:26
  196.1 4.6 %collective-permute-done.1 = f32[16,512]{1,0:T(8,128)S(1)} collective-permute-done((f32[16,512]{1,0:T(8,128)S(1)}, f32[16,512]{1,0:T(8,128)S(1)}, u32[]{:S(2)}, u32[]{:S(2)}) %collective-permute-start.1) | collective-permute-done | bytes 32800 | tf_op jit(solution)/shard_map/while/body/eval_jaxpr/ppermute | solution.py:13
  200.7 4.7 %all_gather.69 = f32[16,1024]{1,0:T(8,128)S(1)} all-gather(f32[16,512]{1,0:T(8,128)S(1)} %get-tuple-element.47), channel_id=1, replica_groups=mesh['group'=2,'tm'=4,'mode'=2,'col'=2] {'mode'}, dimensions={1}, use_global_device_ids=true | all-gather | bytes 98304 | tf_op jit(solution)/shard_map/all_gather | solution.py:26
  208.5 4.3 %collective-permute-done.4 = bf16[16,512]{1,0:T(8,128)(2,1)S(1)} collective-permute-done((bf16[16,512]{1,0:T(8,128)(2,1)S(1)}, bf16[16,512]{1,0:T(8,128)(2,1)S(1)}, u32[]{:S(2)}, u32[]{:S(2)}) %collective-permute-start.4) | collective-permute-done | bytes 16416 | tf_op jit(solution)/shard_map/ppermute | solution.py:13
  212.8 4.4 %all-gather.9 = bf16[16,1024]{1,0:T(8,128)(2,1)S(1)} all-gather(bf16[16,512]{1,0:T(8,128)(2,1)S(1)} %collective-permute-done.4), channel_id=11, replica_groups=mesh['group'=2,'tm'=4,'mode'=2,'col'=2] {'mode'}, dimensions={1}, use_global_device_ids=true | all-gather | bytes 49152 | tf_op jit(solution)/shard_map/all_gather | solution.py:81
  218.7 4.4 %all-gather.10 = bf16[16,1024]{1,0:T(8,128)(2,1)S(1)} all-gather(bf16[16,512]{1,0:T(8,128)(2,1)S(1)} %get-tuple-element.80), channel_id=12, replica_groups=mesh['group'=2,'tm'=4,'mode'=2,'col'=2] {'mode'}, dimensions={1}, use_global_device_ids=true | all-gather | bytes 49152 | tf_op jit(solution)/shard_map/all_gather | solution.py:81
  223.3 4.4 %all-gather.11 = bf16[16,1024]{1,0:T(8,128)(2,1)S(1)} all-gather(bf16[16,512]{1,0:T(8,128)(2,1)S(1)} %get-tuple-element.82), channel_id=13, replica_groups=mesh['group'=2,'tm'=4,'mode'=2,'col'=2] {'mode'}, dimensions={1}, use_global_device_ids=true | all-gather | bytes 49152 | tf_op jit(solution)/shard_map/all_gather | solution.py:81
  (81 shorter events, 68.9 us)
Async XLA Ops:
  7.2 18.5 %copy-start.9 = (bf16[4,16,512]{2,1,0:T(8,128)(2,1)S(1)}, bf16[4,16,512]{2,1,0:T(8,128)(2,1)}, u32[]{:S(2)}) copy-start(bf16[4,16,512]{2,1,0:T(8,128)(2,1)} %param.14) | copy-start | bytes 196612
  7.2 18.5 %copy-start.6 = (bf16[16,512]{1,0:T(8,128)(2,1)S(1)}, bf16[16,512]{1,0:T(8,128)(2,1)}, u32[]{:S(2)}) copy-start(bf16[16,512]{1,0:T(8,128)(2,1)} %param.15) | copy-start | bytes 49156
  7.2 18.5 %copy-start.1 = (bf16[512,1024]{1,0:T(8,128)(2,1)S(1)}, bf16[512,1024]{1,0:T(8,128)(2,1)}, u32[]{:S(2)}) copy-start(bf16[512,1024]{1,0:T(8,128)(2,1)} %param.19) | copy-start | bytes 3145732
  7.2 18.5 %copy-start = (bf16[512,1024]{1,0:T(8,128)(2,1)S(1)}, bf16[512,1024]{1,0:T(8,128)(2,1)}, u32[]{:S(2)}) copy-start(bf16[512,1024]{1,0:T(8,128)(2,1)} %param.20) | copy-start | bytes 3145732
  30.5 9.2 %copy-start.8 = (f32[1,16,512]{2,1,0:T(8,128)S(1)}, f32[1,16,512]{2,1,0:T(8,128)}, u32[]{:S(2)}) copy-start(f32[1,16,512]{2,1,0:T(8,128)} %param.18) | copy-start | bytes 98308
  35.7 21.6 %collective-permute-start.2 = (f32[16,512]{1,0:T(8,128)S(1)}, f32[16,512]{1,0:T(8,128)S(1)}, u32[]{:S(2)}, u32[]{:S(2)}) collective-permute-start(f32[16,512]{1,0:T(8,128)S(1)} %convolution_add_fusion.13), channel_id=1, source_target_pairs={{0,4},{4,8},{8,12},{1,5},{5,9},{9,13},{2,6},{6,10},{10,14},{3,7},{... | collective-permute-start | bytes 98312 | tf_op jit(solution)/shard_map/ppermute | solution.py:13
  39.8 13.1 %collective-permute-start.3 = (bf16[16,512]{1,0:T(8,128)(2,1)S(1)}, bf16[16,512]{1,0:T(8,128)(2,1)S(1)}, u32[]{:S(2)}, u32[]{:S(2)}) collective-permute-start(bf16[16,512]{1,0:T(8,128)(2,1)S(1)} %bitcast_convert_fusion.1), channel_id=1, source_target_pairs={{4,0},{8,4},{12,8},{5,1},{9,5},{13,9},{6,2},{10,6},{14,10},{7,3},{... | collective-permute-start | bytes 49160 | tf_op jit(solution)/shard_map/ppermute | solution.py:13
  42.4 70.9 %all-to-all-start.1 = ((bf16[512,2,512]{0,2,1:T(8,128)(2,1)}), bf16[512,2,512]{0,2,1:T(8,128)(2,1)}, u32[]{:S(2)}, u32[]{:S(2)}) async-start(bf16[512,2,512]{0,2,1:T(8,128)(2,1)} %bitcast.27), calls=%async_computation.1 | async-start | bytes 2097152 | tf_op jit(solution)/shard_map/all_to_all | solution.py:67
  46.8 158.6 %all-gather.14.cloned.1.call-start = ((), (), s32[]{:S(2)}) async-start(), calls=%async_computation.3 | async-start | bytes 3145728 | tf_op jit(solution)/shard_map/all_gather | solution.py:69
  51.3 6.0 %copy-start.7 = (f32[1,16,512]{2,1,0:T(8,128)S(1)}, f32[1,16,512]{2,1,0:T(8,128)}, u32[]{:S(2)}) copy-start(f32[1,16,512]{2,1,0:T(8,128)} %param.17) | copy-start | bytes 98308
  63.7 6.6 %collective-permute-start = (f32[16,512]{1,0:T(8,128)S(1)}, f32[16,512]{1,0:T(8,128)S(1)}, u32[]{:S(2)}, u32[]{:S(2)}) collective-permute-start(f32[16,512]{1,0:T(8,128)S(1)} %convolution_add_fusion.18), channel_id=1, source_target_pairs={{0,4},{4,8},{8,12},{1,5},{5,9},{9,13},{2,6},{6,10},{10,14},{3,7},{... | collective-permute-start | bytes 98312 | tf_op jit(solution)/shard_map/while/body/eval_jaxpr/ppermute | solution.py:13
  77.5 5.8 %collective-permute-start = (f32[16,512]{1,0:T(8,128)S(1)}, f32[16,512]{1,0:T(8,128)S(1)}, u32[]{:S(2)}, u32[]{:S(2)}) collective-permute-start(f32[16,512]{1,0:T(8,128)S(1)} %convolution_add_fusion.18), channel_id=1, source_target_pairs={{0,4},{4,8},{8,12},{1,5},{5,9},{9,13},{2,6},{6,10},{10,14},{3,7},{... | collective-permute-start | bytes 98312 | tf_op jit(solution)/shard_map/while/body/eval_jaxpr/ppermute | solution.py:13
  89.7 5.8 %collective-permute-start = (f32[16,512]{1,0:T(8,128)S(1)}, f32[16,512]{1,0:T(8,128)S(1)}, u32[]{:S(2)}, u32[]{:S(2)}) collective-permute-start(f32[16,512]{1,0:T(8,128)S(1)} %convolution_add_fusion.18), channel_id=1, source_target_pairs={{0,4},{4,8},{8,12},{1,5},{5,9},{9,13},{2,6},{6,10},{10,14},{3,7},{... | collective-permute-start | bytes 98312 | tf_op jit(solution)/shard_map/while/body/eval_jaxpr/ppermute | solution.py:13
  107.1 9.8 %copy-start.2 = (bf16[512,1024]{1,0:T(8,128)(2,1)S(1)}, bf16[512,1024]{1,0:T(8,128)(2,1)}, u32[]{:S(2)}) copy-start(bf16[512,1024]{1,0:T(8,128)(2,1)} %param.19) | copy-start | bytes 3145732
  113.3 19.9 %all-to-all-start.2 = ((bf16[512,2,512]{0,2,1:T(8,128)(2,1)}), bf16[512,2,512]{0,2,1:T(8,128)(2,1)S(1)}, u32[]{:S(2)}, u32[]{:S(2)}) async-start(bf16[512,2,512]{0,2,1:T(8,128)(2,1)} %bitcast.28), calls=%async_computation.2 | async-start | bytes 2097152 | tf_op jit(solution)/shard_map/all_to_all | solution.py:66
  116.9 15.7 %copy-start.10 = (bf16[4,16,512]{2,1,0:T(8,128)(2,1)S(1)}, bf16[4,16,512]{2,1,0:T(8,128)(2,1)}, u32[]{:S(2)}) copy-start(bf16[4,16,512]{2,1,0:T(8,128)(2,1)} %param.16) | copy-start | bytes 196612
  133.2 1.0 copy-start.5
  134.2 31.5 %all-to-all-start = ((f32[512,2,512]{2,0,1:T(8,128)}), f32[512,2,512]{2,0,1:T(8,128)S(1)}, u32[]{:S(2)}, u32[]{:S(2)}) async-start(f32[512,2,512]{2,0,1:T(8,128)} %bitcast.186), calls=%async_computation | async-start | bytes 4194304 | tf_op jit(solution)/shard_map/all_to_all | solution.py:73
  148.9 16.6 %copy-start.4 = (bf16[2,512,512]{2,1,0:T(8,128)(2,1)S(1)}, bf16[2,512,512]{2,1,0:T(8,128)(2,1)}, u32[]{:S(2)}) copy-start(bf16[2,512,512]{2,1,0:T(8,128)(2,1)} %copy.19) | copy-start | bytes 3145732
  171.8 5.8 %collective-permute-start.1 = (f32[16,512]{1,0:T(8,128)S(1)}, f32[16,512]{1,0:T(8,128)S(1)}, u32[]{:S(2)}, u32[]{:S(2)}) collective-permute-start(f32[16,512]{1,0:T(8,128)S(1)} %convolution_add_fusion.19), channel_id=1, source_target_pairs={{4,0},{8,4},{12,8},{5,1},{9,5},{13,9},{6,2},{10,6},{14,10},{7,3},{... | collective-permute-start | bytes 98312 | tf_op jit(solution)/shard_map/while/body/eval_jaxpr/ppermute | solution.py:13
  183.3 5.8 %collective-permute-start.1 = (f32[16,512]{1,0:T(8,128)S(1)}, f32[16,512]{1,0:T(8,128)S(1)}, u32[]{:S(2)}, u32[]{:S(2)}) collective-permute-start(f32[16,512]{1,0:T(8,128)S(1)} %convolution_add_fusion.19), channel_id=1, source_target_pairs={{4,0},{8,4},{12,8},{5,1},{9,5},{13,9},{6,2},{10,6},{14,10},{7,3},{... | collective-permute-start | bytes 98312 | tf_op jit(solution)/shard_map/while/body/eval_jaxpr/ppermute | solution.py:13
  194.8 5.9 %collective-permute-start.1 = (f32[16,512]{1,0:T(8,128)S(1)}, f32[16,512]{1,0:T(8,128)S(1)}, u32[]{:S(2)}, u32[]{:S(2)}) collective-permute-start(f32[16,512]{1,0:T(8,128)S(1)} %convolution_add_fusion.19), channel_id=1, source_target_pairs={{4,0},{8,4},{12,8},{5,1},{9,5},{13,9},{6,2},{10,6},{14,10},{7,3},{... | collective-permute-start | bytes 98312 | tf_op jit(solution)/shard_map/while/body/eval_jaxpr/ppermute | solution.py:13
  200.7 22.4 %copy-start.3 = (bf16[2,512,512]{2,1,0:T(8,128)(2,1)S(1)}, bf16[2,512,512]{2,1,0:T(8,128)(2,1)}, u32[]{:S(2)}) copy-start(bf16[2,512,512]{2,1,0:T(8,128)(2,1)} %copy.17) | copy-start | bytes 3145732
  207.2 5.6 %collective-permute-start.4 = (bf16[16,512]{1,0:T(8,128)(2,1)S(1)}, bf16[16,512]{1,0:T(8,128)(2,1)S(1)}, u32[]{:S(2)}, u32[]{:S(2)}) collective-permute-start(bf16[16,512]{1,0:T(8,128)(2,1)S(1)} %bitcast_convert_fusion), channel_id=1, source_target_pairs={{4,0},{8,4},{12,8},{5,1},{9,5},{13,9},{6,2},{10,6},{14,10},{7,3},{... | collective-permute-start | bytes 49160 | tf_op jit(solution)/shard_map/ppermute | solution.py:13
Sparse Core Ops, SparseCore 0:
  49.2 36.9 all-gather.13
where the time goes:
time: 237 us; the launch traced here: 235 us
  blocking collectives  112 us (47%)
  starting transfers between devices  35.8 us (15%)
  matrix products  23.4 us (10%)
  waiting for transfers between devices  23.4 us (10%)
  between operations  19.2 us (8%)
  local copies, waits for them, and re-layouts  15.2 us (6%)
  other arithmetic  7.06 us (3%)
    all_gather x7, blocking collectives, forward_product(): lax.all_gather(current.astype(jnp.bfloat16), 'mode', axis=2, tiled=True)  42.4 us
    all_gather x7, blocking collectives, backward_product(): lax.all_gather(current.astype(jnp.bfloat16), 'mode', axis=2, tiled=True)  31 us
    ppermute x9, starting transfers between devices, from_behind(): return lax.ppermute(block, axis, route)  23.9 us
    ppermute x9, waiting for transfers between devices, from_behind(): return lax.ppermute(block, axis, route)  22.7 us
    all_gather x4, blocking collectives, coarse_forward(): gathered = lax.all_gather(error_rows, 'mode', axis=1, tiled=True)  19.3 us
    all_gather x4, blocking collectives, coarse_backward(): gathered = lax.all_gather(error_rows, 'mode', axis=1, tiled=True)  18.8 us
    dot_general x4, matrix products, coarse_forward(): return jnp.einsum('cm,rm->cr', gathered, matrix_rows, precision=EXACT)  7.61 us
    select_n x4, local copies, waits for them, and re-layouts, pick_mats(): jnp.where(flag_column[:, None, None] == 1, eclipse_part[None], sun_part[N...  7.46 us
  transfers between devices with their start and end apart: 13, of which 7 were waited for; matrix products, arithmetic and copies ran while one was open for 15% of the time, Pallas kernels for 0%

commit v1 on v0

v1 whole, which is shorter than its diff:
```python
import functools

import jax
import jax.numpy as jnp
from jax import lax
from jax.experimental import pallas as pl
from jax.experimental.pallas import tpu as pltpu
from jax.sharding import PartitionSpec as P

OBJ_WEIGHT = 0.0625
MESH = pl.DeviceIdType.MESH
BF16 = jnp.bfloat16
F32 = jnp.float32
TILE = 256
NT_DIMS = (((1,), (1,)), ((), ()))
NN_DIMS = (((1,), (0,)), ((), ()))


def remote(src, dst, send, recv, **where):
    return pltpu.make_async_remote_copy(
        src_ref=src, dst_ref=dst, send_sem=send, recv_sem=recv, device_id=where, device_id_type=MESH
    )


def times_transposed(rows, tile_of, modes):
    parts = []
    for j in range(modes // TILE):
        tile = tile_of(pl.ds(j * TILE, TILE), slice(None))
        parts.append(lax.dot_general(rows, tile, NT_DIMS, preferred_element_type=F32))
    return jnp.concatenate(parts, axis=1)


def times_plain(rows, tile_of, modes):
    parts = []
    for j in range(modes // TILE):
        tile = tile_of(slice(None), pl.ds(j * TILE, TILE))
        parts.append(lax.dot_general(rows, tile, NN_DIMS, preferred_element_type=F32))
    return jnp.concatenate(parts, axis=1)


def pieces(value):
    hi = value.astype(BF16)
    rest = value - hi.astype(F32)
    mid = rest.astype(BF16)
    lo = (rest - mid.astype(F32)).astype(BF16)
    return jnp.concatenate([hi, mid, lo], axis=0)


def collect(product, cols):
    return product[:cols] + product[cols : 2 * cols] + product[2 * cols :]


def kernel(
    modes_n,
    times_n,
    chunks,
    flags,
    base,
    solar,
    target,
    state,
    adjoint,
    sun,
    eclipse,
    coarse,
    traj_out,
    path_out,
    mats,
    cmat,
    base_f,
    solar_f,
    target_f,
    state_f,
    adj_f,
    state_next,
    adj_next,
    traj,
    path,
    res_f,
    res_b,
    corr,
    own_sem,
    small_send,
    small_recv,
    next_send,
    next_recv,
    one_send,
    one_recv,
    y_send,
    y_recv,
    c_send,
    c_recv,
    d_send,
    d_recv,
    rf_send,
    rf_recv,
    rb_send,
    rb_recv,
):
    g = lax.axis_index("group")
    t = lax.axis_index("tm")
    m = lax.axis_index("mode")
    c = lax.axis_index("col")
    rows = sun.shape[0]
    modes = sun.shape[1]
    steps, cols = base.shape[0], base.shape[1]
    quarter = rows // 4
    piece = quarter // chunks
    mate = 1 - c
    twin = 1 - g

    def lanes(index):
        return pl.ds(pl.multiple_of(index * rows, 128), rows)

    mine = lanes(m)

    own = [
        (state.at[0], state_f.at[:, mine]),
        (base, base_f.at[:, :, mine]),
        (solar, solar_f.at[:, mine]),
        (sun, mats.at[0, pl.ds(pl.multiple_of(m * rows, 16), rows), :]),
        (eclipse, mats.at[1, pl.ds(pl.multiple_of(m * rows, 16), rows), :]),
        (target, target_f.at[:, :, mine]),
        (adjoint.at[0], adj_f.at[:, mine]),
        (coarse, cmat.at[pl.ds(pl.multiple_of(m * rows, 16), rows), :]),
    ]
    own_copies = [pltpu.make_async_copy(s, d, own_sem.at[i]) for i, (s, d) in enumerate(own)]
    for copy in own_copies:
        copy.start()

    barrier = pltpu.get_barrier_semaphore()
    pl.semaphore_signal(barrier, inc=1, device_id={"col": mate}, device_id_type=MESH)
    pl.semaphore_signal(barrier, inc=1, device_id={"group": twin}, device_id_type=MESH)
    for d in range(1, modes_n):
        pl.semaphore_signal(barrier, inc=1, device_id={"mode": lax.rem(m + d, modes_n)}, device_id_type=MESH)
    for d in range(1, times_n):
        pl.semaphore_signal(barrier, inc=1, device_id={"tm": lax.rem(t + d, times_n)}, device_id_type=MESH)
    pl.semaphore_wait(barrier, modes_n + times_n)

    def peer(d):
        return lax.rem(m + d, modes_n)

    def source(d):
        return lax.rem(m + modes_n - d, modes_n)

    small_srcs = [state.at[0], base, solar, target, adjoint.at[0]]

    def small_dst(kind, where):
        if kind == 0:
            return state_f.at[:, where]
        if kind == 1:
            return base_f.at[:, :, where]
        if kind == 2:
            return solar_f.at[:, where]
        if kind == 3:
            return target_f.at[:, :, where]
        return adj_f.at[:, where]

    def small(kind, d):
        at = kind * (modes_n - 1) + d - 1
        return remote(
            small_srcs[kind], small_dst(kind, mine), small_send.at[at], small_recv.at[at], mode=peer(d)
        )

    mat_srcs = [sun, eclipse, coarse]

    def mat_rows(k, start):
        where = pl.ds(pl.multiple_of(start, 16), piece)
        if k < 2:
            return mats.at[k, where, :]
        return cmat.at[where, :]

    order = []
    for k in range(3):
        for q in range(chunks):
            for d in range(1, modes_n):
                order.append((k, q, d))

    part = (g * 2 + c) * quarter
    twin_part = (twin * 2 + c) * quarter

    def first(at):
        k, q, d = order[at]
        inside = part + q * piece
        return remote(
            mat_srcs[k].at[pl.ds(pl.multiple_of(inside, 16), piece), :],
            mat_rows(k, m * rows + inside),
            one_send.at[at],
            one_recv.at[at],
            mode=peer(d),
        )

    def arrived_rows(at, owner_part):
        k, q, d = order[at]
        return mat_rows(k, source(d) * rows + owner_part + q * piece)

    def to_twin(at):
        ref = arrived_rows(at, part)
        return remote(ref, ref, y_send.at[at], y_recv.at[at], group=twin)

    def to_mate(at):
        ref = arrived_rows(at, part)
        return remote(ref, ref, c_send.at[at], c_recv.at[at], col=mate)

    def twin_to_mate(at):
        ref = arrived_rows(at, twin_part)
        return remote(ref, ref, d_send.at[at], d_recv.at[at], col=mate)

    per_mat = chunks * (modes_n - 1)

    def start_small(kinds):
        for kind in kinds:
            for d in range(1, modes_n):
                small(kind, d).start()

    start_small((0, 1, 2))
    for at in range(2 * per_mat):
        first(at).start()
    start_small((4, 3))
    for at in range(2 * per_mat, 3 * per_mat):
        first(at).start()

    def wait_small(kind):
        for d in range(1, modes_n):
            small(kind, d).wait_recv()

    back_down = lax.rem(t + times_n - 1, times_n)

    def next_copy(index):
        src, dst = ((state_f, state_next), (adj_f, adj_next))[index]
        return remote(src, dst, next_send.at[index], next_recv.at[index], tm=back_down)

    own_copies[0].wait()
    wait_small(0)

    @pl.when(t > 0)
    def _():
        next_copy(0).start()

    def relay(first_at, last_at):
        for at in range(first_at, last_at + 1):
            if at < last_at:
                first(at).wait_recv()
                to_twin(at).start()
                to_mate(at).start()
            if at > first_at:
                to_twin(at - 1).wait_recv()
                twin_to_mate(at - 1).start()

    def settle(first_at, last_at):
        for at in range(first_at, last_at):
            to_mate(at).wait_recv()
            twin_to_mate(at).wait_recv()

    relay(0, 2 * per_mat)
    for index in (1, 2, 3, 4):
        own_copies[index].wait()
    wait_small(1)
    wait_small(2)
    settle(0, 2 * per_mat)

    def forcing(n):
        sun_on = (1 - flags[n]).astype(F32)
        return base_f[n].astype(F32) + sun_on * solar_f[...].astype(F32)

    def forward(n, w):
        flag = flags[n]
        return times_transposed(w.astype(BF16), lambda a, b: mats[flag, a, b], modes) + forcing(n)

    ends = lax.fori_loop(0, steps, forward, state_f[...])

    @pl.when(t < times_n - 1)
    def _():
        next_copy(0).wait_recv()
        res_f[t + 1] = ends - state_next[...]

    def res_copy(k):
        slot = lax.rem(t + 1, times_n)
        return remote(
            res_f.at[slot], res_f.at[slot], rf_send.at[k - 1], rf_recv.at[slot], tm=lax.rem(t + k, times_n)
        )

    for k in range(times_n - 1, 0, -1):

        @pl.when(t + k < times_n)
        def _():
            res_copy(k).start()

    own_copies[6].wait()
    wait_small(4)

    @pl.when(t > 0)
    def _():
        next_copy(1).start()

    relay(2 * per_mat, 3 * per_mat)
    own_copies[5].wait()
    own_copies[7].wait()
    wait_small(3)
    settle(2 * per_mat, 3 * per_mat)

    def wait_res(j):
        remote(res_f.at[j], res_f.at[j], rf_send.at[0], rf_recv.at[j], tm=t).wait_recv()

    corr[...] = jnp.zeros_like(corr)

    @pl.when(t >= 1)
    def _():
        wait_res(1)
        corr[...] = res_f[1]

    def coarse_up(j, carry):
        wait_res(j)
        product = times_transposed(pieces(corr[...]), lambda a, b: cmat[a, b], modes)
        corr[...] = collect(product, cols) + res_f[j]
        return carry

    lax.fori_loop(2, t + 1, coarse_up, 0)

    corrected = state_f[...] + corr[...]
    traj[0] = corrected

    def forward_keep(n, w):
        w = forward(n, w)
        traj[n + 1] = w
        return w

    lax.fori_loop(0, steps - 1, forward_keep, corrected)

    def backward(n, w):
        flag = flags[n]
        product = times_plain(w.astype(BF16), lambda a, b: mats[flag, a, b], modes)
        return product + OBJ_WEIGHT * (traj[n] - target_f[n].astype(F32))

    @pl.when(t < times_n - 1)
    def _():
        next_copy(1).wait_recv()

    @pl.when(t == times_n - 1)
    def _():
        adj_next[...] = jnp.zeros_like(adj_next)

    back = lax.fori_loop(0, steps, lambda i, w: backward(steps - 1 - i, w), adj_next[...])
    res_b[t] = back - adj_f[...]

    def back_copy(k):
        return remote(res_b.at[t], res_b.at[t], rb_send.at[k - 1], rb_recv.at[t], tm=lax.rem(t + times_n - k, times_n))

    for k in range(times_n - 1, 0, -1):

        @pl.when(t - k >= 0)
        def _():
            back_copy(k).start()

    traj_out[...] = traj[:, :, mine]

    def wait_back(j):
        remote(res_b.at[j], res_b.at[j], rb_send.at[0], rb_recv.at[j], tm=t).wait_recv()

    @pl.when(t < times_n - 1)
    def _():
        wait_back(times_n - 1)

    corr[...] = res_b[times_n - 1]

    def coarse_down(i, carry):
        j = times_n - 2 - i
        wait_back(j)
        product = times_plain(pieces(corr[...]), lambda a, b: cmat[a, b], modes)
        corr[...] = collect(product, cols) + res_b[j]
        return carry

    lax.fori_loop(0, times_n - 2 - t, coarse_down, 0)

    @pl.when(t < times_n - 1)
    def _():
        later = corr[...]
        adj_next[...] = adj_next[...] + later
        product = times_plain(pieces(later), lambda a, b: cmat[a, b], modes)
        corr[...] = collect(product, cols) + res_b[t]

    path[0] = adj_f[...] + corr[...]

    def backward_keep(i, w):
        n = steps - 1 - i
        w = backward(n, w)
        path[n] = w
        return w

    lax.fori_loop(0, steps - 1, backward_keep, adj_next[...])
    path_out[...] = path[:, :, mine]

    for kind in range(5):
        for d in range(1, modes_n):
            small(kind, d).wait_send()
    for at in range(3 * per_mat):
        first(at).wait_send()
        to_twin(at).wait_send()
        to_mate(at).wait_send()
        twin_to_mate(at).wait_send()

    @pl.when(t > 0)
    def _():
        next_copy(0).wait_send()
        next_copy(1).wait_send()

    for k in range(times_n - 1, 0, -1):

        @pl.when(t + k < times_n)
        def _():
            res_copy(k).wait_send()

        @pl.when(t - k >= 0)
        def _():
            back_copy(k).wait_send()


def local(modes_n, times_n, flags, base, solar, target, state, adjoint, sun, eclipse, coarse):
    rows, modes = sun.shape
    steps, cols = base.shape[0], base.shape[1]
    chunks = max(1, min(4, rows // 4 // 32))
    count = 3 * chunks * (modes_n - 1)
    dma = pltpu.SemaphoreType.DMA
    hbm = pl.BlockSpec(memory_space=pl.ANY)
    vmem = pl.BlockSpec(memory_space=pltpu.VMEM)
    outs = jax.ShapeDtypeStruct((steps, cols, rows), F32)
    return pl.pallas_call(
        functools.partial(kernel, modes_n, times_n, chunks),
        out_shape=(outs, outs),
        in_specs=[pl.BlockSpec(memory_space=pltpu.SMEM)] + [hbm] * 8,
        out_specs=(vmem, vmem),
        scratch_shapes=[
            pltpu.VMEM((2, modes, modes), BF16),
            pltpu.VMEM((modes, modes), BF16),
            pltpu.VMEM((steps, cols, modes), BF16),
            pltpu.VMEM((cols, modes), BF16),
            pltpu.VMEM((steps, cols, modes), BF16),
            pltpu.VMEM((cols, modes), F32),
            pltpu.VMEM((cols, modes), F32),
            pltpu.VMEM((cols, modes), F32),
            pltpu.VMEM((cols, modes), F32),
            pltpu.VMEM((steps, cols, modes), F32),
            pltpu.VMEM((steps, cols, modes), F32),
            pltpu.VMEM((times_n, cols, modes), F32),
            pltpu.VMEM((times_n, cols, modes), F32),
            pltpu.VMEM((cols, modes), F32),
            dma((8,)),
            dma((5 * (modes_n - 1),)),
            dma((5 * (modes_n - 1),)),
            dma((2,)),
            dma((2,)),
            dma((count,)),
            dma((count,)),
            dma((count,)),
            dma((count,)),
            dma((count,)),
            dma((count,)),
            dma((count,)),
            dma((count,)),
            dma((times_n - 1,)),
            dma((times_n,)),
            dma((times_n - 1,)),
            dma((times_n,)),
        ],
        compiler_params=pltpu.CompilerParams(
            collective_id=0, has_side_effects=True, vmem_limit_bytes=32 * 1024 * 1024
        ),
    )(flags, base, solar, target, state, adjoint, sun, eclipse, coarse)


def solution(mesh):
    cells = P(("group", "tm"), "col", "mode")
    in_specs = (
        P(("group", "tm")),
        cells,
        P(("group", "col"), "mode"),
        cells,
        cells,
        cells,
        P("mode", None),
        P("mode", None),
        P("mode", None),
    )
    call = functools.partial(local, mesh.shape["mode"], mesh.shape["tm"])
    return jax.shard_map(call, mesh=mesh, in_specs=in_specs, out_specs=(cells, cells), check_vma=False)
```

time: 237 us -> 65.6 us (0.28)
  blocking collectives: 112 us -> 0 us
  Pallas kernels: 0 us -> 54.8 us
  starting transfers between devices: 35.8 us -> 0 us
  matrix products: 23.4 us -> 0 us
  waiting for transfers between devices: 23.4 us -> 0 us
  between operations: 19.2 us -> 0.66 us
  other arithmetic: 7.06 us -> 0 us
  local copies, waits for them, and re-layouts: 15.2 us -> 9.54 us
    all_gather x22 -> x0, blocking collectives: 112 us -> none  [the longest x7 42.4 us: forward_product(): lax.all_gather(current.astype(jnp.bfloat16), 'mode', axis=2, tiled=True)]
    pallas_call x0 -> x1, Pallas kernels: none -> 54.8 us  [local(): pl.pallas_call(functools.partial(kernel, modes_n, times_n, chunks), out_s...]
    ppermute x9 -> x0, starting transfers between devices: 23.9 us -> none  [from_behind(): return lax.ppermute(block, axis, route)]
    dot_general x22 -> x0, matrix products: 23.4 us -> none  [the longest x4 7.61 us: coarse_forward(): return jnp.einsum('cm,rm->cr', gathered, matrix_rows, precision=EXACT)]
    ppermute x9 -> x0, waiting for transfers between devices: 22.7 us -> none  [from_behind(): return lax.ppermute(block, axis, route)]
    all_to_all x3 -> x0, starting transfers between devices: 11.8 us -> none  [the longest x1 4.44 us: local(): lax.all_to_all(step_eclipse, 'mode', split_axis=1, concat_axis=0, tiled=T...]
    select_n x4 -> x0, local copies, waits for them, and re-layouts: 7.46 us -> none  [pick_mats(): jnp.where(flag_column[:, None, None] == 1, eclipse_part[None], sun_part[N...]
    unnamed x24 -> x20, local copies, waits for them, and re-layouts: 4.69 us -> 9.54 us
  transfers between devices with their start and end apart: 13 -> 0, of which waited for: 7 -> 0; matrix products, arithmetic and copies ran while one was open for 15% -> 0% of each run, Pallas kernels for 0% -> 0%
where the time goes in v1:
time: 65.6 us; the launch traced here: 65 us
  Pallas kernels  54.8 us (84%)
  local copies, waits for them, and re-layouts  9.54 us (15%)
  between operations  0.66 us (1%)
    pallas_call x1, Pallas kernels, local(): pl.pallas_call(functools.partial(kernel, modes_n, times_n, chunks), out_s...  54.8 us
    unnamed x20, local copies, waits for them, and re-layouts  9.54 us

profile of v1, /device:TPU:0, one launch (start us, length us, event | category | flops | bytes accessed | tf_op | source)
XLA Modules:
  0.0 65.0 jit_solution(4378734116028148595)
XLA Ops:
  0.6 0.0 copy-start
  0.6 1.2 %copy-done = bf16[512,1024]{1,0:T(8,128)(2,1)S(1)} copy-done((bf16[512,1024]{1,0:T(8,128)(2,1)S(1)}, bf16[512,1024]{1,0:T(8,128)(2,1)}, u32[]{:S(2)}) %copy-start) | copy-done | bytes 1048600
  1.9 0.0 copy-start.1
  1.9 1.2 %copy-done.1 = bf16[512,1024]{1,0:T(8,128)(2,1)S(1)} copy-done((bf16[512,1024]{1,0:T(8,128)(2,1)S(1)}, bf16[512,1024]{1,0:T(8,128)(2,1)}, u32[]{:S(2)}) %copy-start.1) | copy-done | bytes 1048600
  3.1 0.0 copy-start.2
  3.1 1.2 %copy-done.2 = bf16[512,1024]{1,0:T(8,128)(2,1)S(1)} copy-done((bf16[512,1024]{1,0:T(8,128)(2,1)S(1)}, bf16[512,1024]{1,0:T(8,128)(2,1)}, u32[]{:S(2)}) %copy-start.2) | copy-done | bytes 1048600
  4.3 0.0 copy-start.3
  4.3 0.8 %copy-done.3 = bf16[4,16,512]{2,1,0:T(8,128)(2,1)S(1)} copy-done((bf16[4,16,512]{2,1,0:T(8,128)(2,1)S(1)}, bf16[4,16,512]{2,1,0:T(8,128)(2,1)}, u32[]{:S(2)}) %copy-start.3) | copy-done | bytes 65560
  5.1 0.0 copy-start.4
  5.2 0.8 %copy-done.4 = bf16[4,16,512]{2,1,0:T(8,128)(2,1)S(1)} copy-done((bf16[4,16,512]{2,1,0:T(8,128)(2,1)S(1)}, bf16[4,16,512]{2,1,0:T(8,128)(2,1)}, u32[]{:S(2)}) %copy-start.4) | copy-done | bytes 65560
  6.0 0.0 copy-start.5
  6.0 0.8 %copy-done.5 = f32[1,16,512]{2,1,0:T(8,128)S(1)} copy-done((f32[1,16,512]{2,1,0:T(8,128)S(1)}, f32[1,16,512]{2,1,0:T(8,128)}, u32[]{:S(2)}) %copy-start.5) | copy-done | bytes 32792
  6.7 0.0 copy-start.6
  6.8 0.8 %copy-done.6 = f32[1,16,512]{2,1,0:T(8,128)S(1)} copy-done((f32[1,16,512]{2,1,0:T(8,128)S(1)}, f32[1,16,512]{2,1,0:T(8,128)}, u32[]{:S(2)}) %copy-start.6) | copy-done | bytes 32792
  7.5 0.0 copy-start.7
  7.5 0.7 %copy-done.7 = bf16[16,512]{1,0:T(8,128)(2,1)S(1)} copy-done((bf16[16,512]{1,0:T(8,128)(2,1)S(1)}, bf16[16,512]{1,0:T(8,128)(2,1)}, u32[]{:S(2)}) %copy-start.7) | copy-done | bytes 16408
  8.2 0.0 copy-start.8
  8.2 0.7 %copy-done.8 = s32[4]{0:T(128)S(1)} copy-done((s32[4]{0:T(128)S(1)}, s32[4]{0:T(128)}, u32[]{:S(2)}) %copy-start.8) | copy-done | bytes 40
  8.9 54.8 %shard_map.104 = (f32[4,16,512]{2,1,0:T(8,128)S(1)}, f32[4,16,512]{2,1,0:T(8,128)S(1)}) custom-call(s32[4]{0:T(128)S(1)} %copy-done.8, bf16[4,16,512]{2,1,0:T(8,128)(2,1)S(1)} %copy-done.3, bf16[16,512]{1,0:T(8,128)(2,1)S(1)} %copy-done.7, bf16[4,16,512]{2,1,0:T(8,128)(2,1)S(1)} %copy-done.4, f32[1,16,512]{2,1,0:T(8,128)S(1)} %copy-done.5, ...), custom_call_target="tpu_custom_call" | custom-call | tf_op jit(solution)/shard_map/pallas_call | solution.py:427
  63.7 0.7 %copy.13 = f32[4,16,512]{2,1,0:T(8,128)} copy(f32[4,16,512]{2,1,0:T(8,128)S(1)} %get-tuple-element.4) | data formatting | bytes 262144
  64.4 0.7 %copy.14 = f32[4,16,512]{2,1,0:T(8,128)} copy(f32[4,16,512]{2,1,0:T(8,128)S(1)} %get-tuple-element.5) | data formatting | bytes 262144
Async XLA Ops:
  0.6 1.2 %copy-start = (bf16[512,1024]{1,0:T(8,128)(2,1)S(1)}, bf16[512,1024]{1,0:T(8,128)(2,1)}, u32[]{:S(2)}) copy-start(bf16[512,1024]{1,0:T(8,128)(2,1)} %sun.1) | copy-start | bytes 3145732
  1.9 1.2 %copy-start.1 = (bf16[512,1024]{1,0:T(8,128)(2,1)S(1)}, bf16[512,1024]{1,0:T(8,128)(2,1)}, u32[]{:S(2)}) copy-start(bf16[512,1024]{1,0:T(8,128)(2,1)} %eclipse.1) | copy-start | bytes 3145732
  3.1 1.2 %copy-start.2 = (bf16[512,1024]{1,0:T(8,128)(2,1)S(1)}, bf16[512,1024]{1,0:T(8,128)(2,1)}, u32[]{:S(2)}) copy-start(bf16[512,1024]{1,0:T(8,128)(2,1)} %coarse.1) | copy-start | bytes 3145732
  4.3 0.8 %copy-start.3 = (bf16[4,16,512]{2,1,0:T(8,128)(2,1)S(1)}, bf16[4,16,512]{2,1,0:T(8,128)(2,1)}, u32[]{:S(2)}) copy-start(bf16[4,16,512]{2,1,0:T(8,128)(2,1)} %base.1) | copy-start | bytes 196612
  5.1 0.8 %copy-start.4 = (bf16[4,16,512]{2,1,0:T(8,128)(2,1)S(1)}, bf16[4,16,512]{2,1,0:T(8,128)(2,1)}, u32[]{:S(2)}) copy-start(bf16[4,16,512]{2,1,0:T(8,128)(2,1)} %target.1) | copy-start | bytes 196612
  6.0 0.8 %copy-start.5 = (f32[1,16,512]{2,1,0:T(8,128)S(1)}, f32[1,16,512]{2,1,0:T(8,128)}, u32[]{:S(2)}) copy-start(f32[1,16,512]{2,1,0:T(8,128)} %state.1) | copy-start | bytes 98308
  6.7 0.8 %copy-start.6 = (f32[1,16,512]{2,1,0:T(8,128)S(1)}, f32[1,16,512]{2,1,0:T(8,128)}, u32[]{:S(2)}) copy-start(f32[1,16,512]{2,1,0:T(8,128)} %adjoint.1) | copy-start | bytes 98308
  7.5 0.7 %copy-start.7 = (bf16[16,512]{1,0:T(8,128)(2,1)S(1)}, bf16[16,512]{1,0:T(8,128)(2,1)}, u32[]{:S(2)}) copy-start(bf16[16,512]{1,0:T(8,128)(2,1)} %solar.1) | copy-start | bytes 49156
  8.2 0.7 %copy-start.8 = (s32[4]{0:T(128)S(1)}, s32[4]{0:T(128)}, u32[]{:S(2)}) copy-start(s32[4]{0:T(128)} %flags.1) | copy-start | bytes 52

commit v2 on v1

--- a/solution.py
+++ b/solution.py
@@ -92,6 +92,8 @@
     c_recv,
     d_send,
     d_recv,
+    far_low,
+    far_high,
     rf_send,
     rf_recv,
     rb_send,
@@ -133,9 +135,39 @@
     pl.semaphore_signal(barrier, inc=1, device_id={"group": twin}, device_id_type=MESH)
     for d in range(1, modes_n):
         pl.semaphore_signal(barrier, inc=1, device_id={"mode": lax.rem(m + d, modes_n)}, device_id_type=MESH)
-    for d in range(1, times_n):
-        pl.semaphore_signal(barrier, inc=1, device_id={"tm": lax.rem(t + d, times_n)}, device_id_type=MESH)
-    pl.semaphore_wait(barrier, modes_n + times_n)
+
+    def signal_tm(semaphore, where):
+        pl.semaphore_signal(semaphore, inc=1, device_id={"tm": where}, device_id_type=MESH)
+
+    @pl.when(t > 0)
+    def _():
+        signal_tm(barrier, t - 1)
+
+    @pl.when(t < times_n - 1)
+    def _():
+        signal_tm(barrier, t + 1)
+
+    has_low = lax.div(t + times_n - 1, times_n)
+    has_high = lax.div(2 * times_n - 2 - t, times_n)
+    pl.semaphore_wait(barrier, modes_n + 1 + has_low + has_high)
+
+    def pass_on(entry):
+        @pl.when(jnp.logical_and(t - 1 - entry >= 0, t + 1 < times_n))
+        def _():
+            signal_tm(far_low.at[entry], t + 1)
+
+        @pl.when(jnp.logical_and(t + 1 + entry < times_n, t - 1 >= 0))
+        def _():
+            signal_tm(far_high.at[entry], t - 1)
+
+    def hear(entry):
+        @pl.when(t - 2 - entry >= 0)
+        def _():
+            pl.semaphore_wait(far_low.at[entry], 1)
+
+        @pl.when(t + 2 + entry < times_n)
+        def _():
+            pl.semaphore_wait(far_high.at[entry], 1)
 
     def peer(d):
         return lax.rem(m + d, modes_n)
@@ -213,13 +245,16 @@
             for d in range(1, modes_n):
                 small(kind, d).start()
 
-    start_small((0, 1, 2))
     for at in range(2 * per_mat):
         first(at).start()
+    start_small((0, 1, 2))
     start_small((4, 3))
     for at in range(2 * per_mat, 3 * per_mat):
         first(at).start()
 
+    if times_n > 2:
+        pass_on(0)
+
     def wait_small(kind):
         for d in range(1, modes_n):
             small(kind, d).wait_recv()
@@ -229,13 +264,6 @@
     def next_copy(index):
         src, dst = ((state_f, state_next), (adj_f, adj_next))[index]
         return remote(src, dst, next_send.at[index], next_recv.at[index], tm=back_down)
-
-    own_copies[0].wait()
-    wait_small(0)
-
-    @pl.when(t > 0)
-    def _():
-        next_copy(0).start()
 
     def relay(first_at, last_at):
         for at in range(first_at, last_at + 1):
@@ -253,6 +281,13 @@
             twin_to_mate(at).wait_recv()
 
     relay(0, 2 * per_mat)
+    own_copies[0].wait()
+    wait_small(0)
+
+    @pl.when(t > 0)
+    def _():
+        next_copy(0).start()
+
     for index in (1, 2, 3, 4):
         own_copies[index].wait()
     wait_small(1)
@@ -273,6 +308,11 @@
     def _():
         next_copy(0).wait_recv()
         res_f[t + 1] = ends - state_next[...]
+
+    for entry in range(times_n - 2):
+        hear(entry)
+        if entry + 1 < times_n - 2:
+            pass_on(entry + 1)
 
     def res_copy(k):
         slot = lax.rem(t + 1, times_n)
@@ -418,7 +458,7 @@
 def local(modes_n, times_n, flags, base, solar, target, state, adjoint, sun, eclipse, coarse):
     rows, modes = sun.shape
     steps, cols = base.shape[0], base.shape[1]
-    chunks = max(1, min(4, rows // 4 // 32))
+    chunks = max(1, min(2, rows // 4 // 32))
     count = 3 * chunks * (modes_n - 1)
     dma = pltpu.SemaphoreType.DMA
     hbm = pl.BlockSpec(memory_space=pl.ANY)
@@ -457,13 +497,15 @@
             dma((count,)),
             dma((count,)),
             dma((count,)),
+            pltpu.SemaphoreType.REGULAR((max(1, times_n - 2),)),
+            pltpu.SemaphoreType.REGULAR((max(1, times_n - 2),)),
             dma((times_n - 1,)),
             dma((times_n,)),
             dma((times_n - 1,)),
             dma((times_n,)),
         ],
         compiler_params=pltpu.CompilerParams(
-            collective_id=0, has_side_effects=True, vmem_limit_bytes=32 * 1024 * 1024
+            collective_id=0, has_side_effects=True, vmem_limit_bytes=60 * 1024 * 1024
         ),
     )(flags, base, solar, target, state, adjoint, sun, eclipse, coarse)
 

time: 65.6 us -> 53.3 us (0.81)
  local copies, waits for them, and re-layouts: 9.54 us -> 2.26 us
  Pallas kernels: 54.8 us -> 50.3 us
    unnamed x20 -> x4, local copies, waits for them, and re-layouts: 9.54 us -> 2.26 us
    pallas_call x1, Pallas kernels: 54.8 us -> 50.3 us  [local(): pl.pallas_call(functools.partial(kernel, modes_n, times_n, chunks), out_s...]
where the time goes in v2:
time: 53.3 us; the launch traced here: 53.2 us
  Pallas kernels  50.3 us (94%)
  local copies, waits for them, and re-layouts  2.26 us (4%)
  between operations  0.65 us (1%)
    pallas_call x1, Pallas kernels, local(): pl.pallas_call(functools.partial(kernel, modes_n, times_n, chunks), out_s...  50.3 us
    unnamed x4, local copies, waits for them, and re-layouts  2.26 us

profile of v2, /device:TPU:0, one launch (start us, length us, event | category | flops | bytes accessed | tf_op | source)
XLA Modules:
  0.0 53.2 jit_solution(652666953331223219)
XLA Ops:
  0.6 50.3 %shard_map.104 = (f32[4,16,512]{2,1,0:T(8,128)}, f32[4,16,512]{2,1,0:T(8,128)}) custom-call(s32[4]{0:T(128)} %flags.1, bf16[4,16,512]{2,1,0:T(8,128)(2,1)} %base.1, bf16[16,512]{1,0:T(8,128)(2,1)} %solar.1, bf16[4,16,512]{2,1,0:T(8,128)(2,1)} %target.1, f32[1,16,512]{2,1,0:T(8,128)} %state.1, f32[1,16,512]{2,1,0:T(8,128)} %adjoint.1, bf16[512,1024]{1,0:T(8,128)(2,1)} %sun.1, ...), custom_call_target="tpu_custom_call" | custom-call | tf_op jit(solution)/shard_map/pallas_call | solution.py:467
  50.9 0.0 copy-start
  50.9 1.6 %copy.13 = f32[4,16,512]{2,1,0:T(8,128)} copy(f32[4,16,512]{2,1,0:T(8,128)} %get-tuple-element.4) | data formatting | bytes 262144
  52.5 0.0 copy-done
  52.5 0.7 %copy.14 = f32[4,16,512]{2,1,0:T(8,128)} copy(f32[4,16,512]{2,1,0:T(8,128)S(1)} %copy-done) | data formatting | bytes 262144
Async XLA Ops:
  50.9 1.6 %copy-start = (f32[4,16,512]{2,1,0:T(8,128)S(1)}, f32[4,16,512]{2,1,0:T(8,128)}, u32[]{:S(2)}) copy-start(f32[4,16,512]{2,1,0:T(8,128)} %get-tuple-element.5) | copy-start | bytes 393220

commit v3 on v2

--- a/solution.py
+++ b/solution.py
@@ -63,8 +63,7 @@
     sun,
     eclipse,
     coarse,
-    traj_out,
-    path_out,
+    both_out,
     mats,
     cmat,
     base_f,
@@ -392,7 +391,7 @@
         def _():
             back_copy(k).start()
 
-    traj_out[...] = traj[:, :, mine]
+    both_out[0] = traj[:, :, mine]
 
     def wait_back(j):
         remote(res_b.at[j], res_b.at[j], rb_send.at[0], rb_recv.at[j], tm=t).wait_recv()
@@ -428,7 +427,7 @@
         return w
 
     lax.fori_loop(0, steps - 1, backward_keep, adj_next[...])
-    path_out[...] = path[:, :, mine]
+    both_out[1] = path[:, :, mine]
 
     for kind in range(5):
         for d in range(1, modes_n):
@@ -463,12 +462,12 @@
     dma = pltpu.SemaphoreType.DMA
     hbm = pl.BlockSpec(memory_space=pl.ANY)
     vmem = pl.BlockSpec(memory_space=pltpu.VMEM)
-    outs = jax.ShapeDtypeStruct((steps, cols, rows), F32)
-    return pl.pallas_call(
+    outs = jax.ShapeDtypeStruct((2, steps, cols, rows), F32)
+    both = pl.pallas_call(
         functools.partial(kernel, modes_n, times_n, chunks),
-        out_shape=(outs, outs),
+        out_shape=outs,
         in_specs=[pl.BlockSpec(memory_space=pltpu.SMEM)] + [hbm] * 8,
-        out_specs=(vmem, vmem),
+        out_specs=vmem,
         scratch_shapes=[
             pltpu.VMEM((2, modes, modes), BF16),
             pltpu.VMEM((modes, modes), BF16),
@@ -508,6 +507,7 @@
             collective_id=0, has_side_effects=True, vmem_limit_bytes=60 * 1024 * 1024
         ),
     )(flags, base, solar, target, state, adjoint, sun, eclipse, coarse)
+    return both[0], both[1]
 
 
 def solution(mesh):

time: 53.3 us -> 52.8 us (level)
  local copies, waits for them, and re-layouts: 2.26 us -> 1.69 us
    unnamed x4 -> x0, local copies, waits for them, and re-layouts: 2.26 us -> none
    squeeze x0 -> x1, local copies, waits for them, and re-layouts: none -> 1.69 us  [local(): return (both[0], both[1])]
where the time goes in v3:
time: 52.8 us; the launch traced here: 52.6 us
  Pallas kernels  50.3 us (95%)
  local copies, waits for them, and re-layouts  1.69 us (3%)
  between operations  0.64 us (1%)
    pallas_call x1, Pallas kernels, local(): pl.pallas_call(functools.partial(kernel, modes_n, times_n, chunks), out_s...  50.3 us
    squeeze x1, local copies, waits for them, and re-layouts, local(): return (both[0], both[1])  1.69 us

profile of v3, /device:TPU:0, one launch (start us, length us, event | category | flops | bytes accessed | tf_op | source)
XLA Modules:
  0.0 52.6 jit_solution(4108801903967358837)
XLA Ops:
  0.6 50.3 %shard_map.104 = f32[2,4,16,512]{3,2,1,0:T(8,128)} custom-call(s32[4]{0:T(128)} %flags.1, bf16[4,16,512]{2,1,0:T(8,128)(2,1)} %base.1, bf16[16,512]{1,0:T(8,128)(2,1)} %solar.1, bf16[4,16,512]{2,1,0:T(8,128)(2,1)} %target.1, f32[1,16,512]{2,1,0:T(8,128)} %state.1, f32[1,16,512]{2,1,0:T(8,128)} %adjoint.1, bf16[512,1024]{1,0:T(8,128)(2,1)} %sun.1, ...), custom_call_target="tpu_custom_call" | custom-call | tf_op jit(solution)/shard_map/pallas_call | solution.py:466
  50.9 1.7 %slice_bitcast_fusion = (f32[4,16,512]{2,1,0:T(8,128)}, f32[4,16,512]{2,1,0:T(8,128)}) fusion(f32[2,4,16,512]{3,2,1,0:T(8,128)} %shard_map.104), kind=kLoop, calls=%fused_computation | loop fusion | bytes 524288 | tf_op jit(solution)/shard_map/squeeze | solution.py:510
